TPU v7x, 32 devices: a whole 2x2x4 slice. The times are simulated.
32 devices in a mesh: dp: 8 (over y, x, core), tensor: 4 (over z).
Axes of the slice: x: 2, y: 2, z: 4, core: 2. Of those that a mesh axis runs over, the one named last changes fastest.
Arguments:
- out_grad: bfloat16 [8, 256, 4096], P('dp', 'tensor'), may hold values from -6 to 6
- out_weight: bfloat16 [4096, 1024], P('dp', 'tensor'), may hold values from -0.1875 to 0.1875
- queries: bfloat16 [8, 256, 1024], P('dp', None, 'tensor'), may hold values from -5 to 5
- keys: bfloat16 [8, 256, 512], P('dp', None, 'tensor'), may hold values from -5 to 5, as said below
- values: bfloat16 [8, 256, 512], P('dp', None, 'tensor'), may hold values from -6 to 6, as said below
- segment_ids: int32 [8, 256], P('dp'), may hold values from 0 to 3, never falling along the last dimension, each value on 1 to 128 neighbouring positions
Outputs:
- d_queries: bfloat16 [8, 256, 1024], P('dp', None, 'tensor')
- d_keys: bfloat16 [8, 256, 512], P('dp', None, 'tensor')
- d_values: bfloat16 [8, 256, 512], P('dp', None, 'tensor')
- d_out_weight: float32 [4096, 1024], P('dp', 'tensor')
Inputs may be any that keep to these rules, and one draw needn't show every extreme that they name: `keys`: column blocks 2 g and 2 g + 1 are equal. `values`: column blocks 2 g and 2 g + 1 are equal.
All inputs are finite; a program needn't handle non-finite values.
Results may differ from a plain program's by a relative error of at most 0.018.
Values may be sent and summed in bfloat16 or wider, within the bound.
A program may use at most 128 MiB of HBM per device.

v0:
```python
import jax
import jax.numpy as jnp
from jax import lax
from jax.sharding import PartitionSpec as P

HD = 128


def from_partner(block, axis, bit):
    count = lax.axis_size(axis)
    route = []
    for low in range(count):
        high = low | 1 << bit
        if high != low and high < count:
            route += [(low, high), (high, low)]
    return lax.ppermute(block, axis, route)


def local(out_grad, out_weight, queries, keys, values, segment_ids):
    scale = HD ** (-0.5)
    grad_local = out_grad[0]
    query_rows = queries[0]
    length = query_rows.shape[0]
    width = query_rows.shape[1]
    heads_here = width // HD
    key_local = keys[0]
    value_local = values[0]
    query_heads = query_rows.reshape(length, heads_here, HD)
    scores = (
        jnp.einsum("qhd,kd->hqk", query_heads, key_local, preferred_element_type=jnp.float32)
        * scale
    )
    segments = segment_ids[0]
    position = jnp.arange(length)
    visible = (segments[:, None] == segments[None, :]) & (position[:, None] >= position[None, :])
    masked = jnp.where(visible[None], scores, -jnp.inf)
    top_score = jnp.max(masked, axis=-1, keepdims=True)
    raw_exp = jnp.exp(masked - top_score)
    attn_prob = raw_exp / jnp.sum(raw_exp, axis=-1, keepdims=True)
    prob_low = attn_prob.astype(jnp.bfloat16)
    attn_out = jnp.einsum(
        "hqk,kd->qhd", prob_low, value_local, preferred_element_type=jnp.float32
    ).astype(jnp.bfloat16)
    flat_out = attn_out.reshape(length, width)
    grad_full = lax.all_gather(grad_local, "tensor", axis=0, tiled=True)
    columns = grad_full
    grad_sum = jnp.dot(
        columns,
        lax.all_gather(out_weight, "dp", axis=0, tiled=True),
        preferred_element_type=jnp.float32,
    )
    columns = grad_full
    weight_rows = lax.psum_scatter(
        lax.dot_general(
            columns, flat_out, (((0,), (0,)), ((), ())), preferred_element_type=jnp.float32
        ).astype(jnp.bfloat16),
        "dp",
        scatter_dimension=0,
        tiled=True,
    ).astype(jnp.float32)
    grad_attn = grad_sum.astype(jnp.bfloat16)
    grad_heads = grad_attn.reshape(length, heads_here, HD)
    deltas = jnp.sum(grad_heads.astype(jnp.float32) * attn_out.astype(jnp.float32), axis=-1)
    grad_values = jnp.einsum(
        "hqk,qhd->kd", prob_low, grad_heads, preferred_element_type=jnp.float32
    )
    grad_prob = jnp.einsum(
        "qhd,kd->hqk", grad_heads, value_local, preferred_element_type=jnp.float32
    )
    grad_score = (attn_prob * (grad_prob - jnp.transpose(deltas)[:, :, None]) * scale).astype(
        jnp.bfloat16
    )
    grad_queries = jnp.einsum(
        "hqk,kd->qhd", grad_score, key_local, preferred_element_type=jnp.float32
    ).astype(jnp.bfloat16)
    grad_keys = jnp.einsum(
        "hqk,qhd->kd", grad_score, query_heads, preferred_element_type=jnp.float32
    )
    partner_keys, partner_values = (
        from_partner(grad_keys.astype(jnp.bfloat16), "tensor", 0).astype(grad_keys.dtype),
        from_partner(grad_values.astype(jnp.bfloat16), "tensor", 0).astype(grad_values.dtype),
    )
    keys_total = (grad_keys + partner_keys).astype(jnp.bfloat16)
    values_total = (grad_values + partner_values).astype(jnp.bfloat16)
    weight_grad = weight_rows / lax.axis_size("dp")
    return (
        grad_queries.reshape(1, length, width),
        keys_total[None],
        values_total[None],
        weight_grad,
    )


def solution(mesh):
    in_specs = (
        P("dp", "tensor", None),
        P("dp", "tensor"),
        P("dp", None, "tensor"),
        P("dp", None, "tensor"),
        P("dp", None, "tensor"),
        P("dp", None),
    )
    out_specs = (
        P("dp", None, "tensor"),
        P("dp", None, "tensor"),
        P("dp", None, "tensor"),
        P("dp", "tensor"),
    )
    return jax.shard_map(local, mesh=mesh, in_specs=in_specs, out_specs=out_specs, check_vma=False)
```

profile of v0, /device:TPU:0, one launch (start us, length us, event | category | flops | bytes accessed | tf_op | source)
XLA Modules:
  0.0 143.6 jit_solution(18421356278678418032)
XLA Ops:
  7.2 0.0 copy-start
  7.2 0.0 all-gather.6.cloned.1.call-start
  7.2 0.7 all-gather.6.cloned.1.call-update
  7.9 0.0 all-gather.4.cloned.1.call-start
  8.0 0.7 all-gather.4.cloned.1.call-update
  8.7 0.0 reduce-scatter.2.cloned.1.call-start
  8.7 0.9 reshape_squeeze.3
  9.7 0.9 fusion.16
  10.5 0.0 copy-done
  10.5 0.3 fusion.55
  10.9 0.0 copy-start.2
  10.9 47.4 %all-gather.6.cloned.1.call-done = bf16[1,256,4096]{2,1,0:T(8,128)(2,1)} async-done(((bf16[1,64,4096]{2,1,0:T(8,128)(2,1)}), bf16[1,256,4096]{2,1,0:T(8,128)(2,1)}) %all-gather.6.cloned.1.call-update) | async-done | bytes 2097168 | tf_op jit(solution)/shard_map/all_gather | solution.py:45
  58.3 28.5 %all-gather.4.cloned.1.call-done = bf16[4096,256]{1,0:T(8,128)(2,1)} async-done(((bf16[512,256]{1,0:T(8,128)(2,1)}), bf16[4096,256]{1,0:T(8,128)(2,1)}) %all-gather.4.cloned.1.call-update) | async-done | bytes 2097168 | tf_op jit(solution)/shard_map/all_gather | solution.py:49
  86.8 3.1 %fusion.13 = bf16[256,256]{0,1:T(8,128)(2,1)S(1)} fusion(bf16[4096,256]{1,0:T(8,128)(2,1)} %all-gather.4.cloned.1.call-done, bf16[1,256,4096]{2,1,0:T(8,128)(2,1)} %all-gather.6.cloned.1.call-done), kind=kOutput, calls=%fused_computation.18 | convolution fusion | flops 536936448 | bytes 4325376 | tf_op jit(solution)/shard_map/dot_general | solution.py:47
  89.9 0.0 copy-start.1
  89.9 0.0 copy-done.2
  90.0 0.5 multiply_reduce_fusion
  90.5 1.0 copy-done.1
  91.5 2.1 %fusion.1 = bf16[4096,256]{0,1:T(8,128)(2,1)} fusion(bf16[256,256]{0,1:T(8,128)(2,1)S(1)} %bitcast.105, bf16[1,256,4096]{2,1,0:T(8,128)(2,1)S(1)} %copy-done.1), kind=kOutput, calls=%fused_computation.2 | convolution fusion | flops 537919488 | bytes 4325376 | tf_op jit(solution)/shard_map/dot_general | solution.py:54
  93.6 0.0 reduce-scatter.2.cloned.1.call-update
  93.6 0.2 fusion.12
  93.8 0.2 fusion.64
  94.1 1.5 %collective-permute-start = (bf16[256,128]{1,0:T(8,128)(2,1)S(1)}, bf16[256,128]{1,0:T(8,128)(2,1)S(1)}, u32[]{:S(2)}, u32[]{:S(2)}) collective-permute-start(bf16[256,128]{1,0:T(8,128)(2,1)S(1)} %get-tuple-element.12), channel_id=1, source_target_pairs={{0,1},{1,0},{2,3},{3,2},{4,5},{5,4},{6,7},{7,6},{8,9},{9,8},{10,11... | collective-permute-start | bytes 196616 | tf_op jit(solution)/shard_map/ppermute | solution.py:16
  95.6 0.2 convolution_convert_fusion.1
  95.8 0.5 fusion.65
  96.4 0.8 copy.19
  97.1 0.5 collective-permute-start.1
  97.7 0.7 collective-permute-done
  98.4 0.6 fusion.20
  99.0 2.3 %collective-permute-done.1 = bf16[256,128]{1,0:T(8,128)(2,1)S(1)} collective-permute-done((bf16[256,128]{1,0:T(8,128)(2,1)S(1)}, bf16[256,128]{1,0:T(8,128)(2,1)S(1)}, u32[]{:S(2)}, u32[]{:S(2)}) %collective-permute-start.1) | collective-permute-done | bytes 65568 | tf_op jit(solution)/shard_map/ppermute | solution.py:16
  101.4 0.6 fusion.21
  102.0 33.0 %reduce-scatter.2.cloned.1.call-done = bf16[512,256]{0,1:T(8,128)(2,1)} async-done(((bf16[4096,256]{0,1:T(8,128)(2,1)}), bf16[512,256]{0,1:T(8,128)(2,1)}) %reduce-scatter.2.cloned.1.call-update) | async-done | bytes 262160 | tf_op jit(solution)/shard_map/reduce_scatter | solution.py:53
  135.0 1.0 convert_multiply_fusion
  136.0 1.0 copy.20
Async XLA Ops:
  7.2 3.4 %copy-start = (bf16[1,256,128]{2,1,0:T(8,128)(2,1)S(1)}, bf16[1,256,128]{2,1,0:T(8,128)(2,1)}, u32[]{:S(2)}) copy-start(bf16[1,256,128]{2,1,0:T(8,128)(2,1)} %param.9) | copy-start | bytes 196612
  7.2 51.1 %all-gather.6.cloned.1.call-start = ((), (), s32[]{:S(2)}) async-start(), calls=%async_computation.3 | async-start | bytes 2621440 | tf_op jit(solution)/shard_map/all_gather | solution.py:45
  7.9 78.9 %all-gather.4.cloned.1.call-start = ((), (), s32[]{:S(2)}) async-start(), calls=%async_computation.1 | async-start | bytes 2359296 | tf_op jit(solution)/shard_map/all_gather | solution.py:49
  8.7 126.3 %reduce-scatter.2.cloned.1.call-start = ((), (), s32[]{:S(2)}) async-start(), calls=%async_computation.2 | async-start | bytes 2359296 | tf_op jit(solution)/shard_map/reduce_scatter | solution.py:53
  10.9 79.1 %copy-start.2 = (bf16[1,256,128]{2,1,0:T(8,128)(2,1)S(1)}, bf16[1,256,128]{2,1,0:T(8,128)(2,1)}, u32[]{:S(2)}) copy-start(bf16[1,256,128]{2,1,0:T(8,128)(2,1)} %param.10) | copy-start | bytes 196612
  89.9 1.6 %copy-start.1 = (bf16[1,256,4096]{2,1,0:T(8,128)(2,1)S(1)}, bf16[1,256,4096]{2,1,0:T(8,128)(2,1)}, u32[]{:S(2)}) copy-start(bf16[1,256,4096]{2,1,0:T(8,128)(2,1)} %all-gather.6.cloned.1.call-done) | copy-start | bytes 6291460
  94.1 4.3 %collective-permute-start = (bf16[256,128]{1,0:T(8,128)(2,1)S(1)}, bf16[256,128]{1,0:T(8,128)(2,1)S(1)}, u32[]{:S(2)}, u32[]{:S(2)}) collective-permute-start(bf16[256,128]{1,0:T(8,128)(2,1)S(1)} %get-tuple-element.12), channel_id=1, source_target_pairs={{0,1},{1,0},{2,3},{3,2},{4,5},{5,4},{6,7},{7,6},{8,9},{9,8},{10,11... | collective-permute-start | bytes 196616 | tf_op jit(solution)/shard_map/ppermute | solution.py:16
  97.1 4.3 %collective-permute-start.1 = (bf16[256,128]{1,0:T(8,128)(2,1)S(1)}, bf16[256,128]{1,0:T(8,128)(2,1)S(1)}, u32[]{:S(2)}, u32[]{:S(2)}) collective-permute-start(bf16[256,128]{1,0:T(8,128)(2,1)S(1)} %get-tuple-element.14), channel_id=1, source_target_pairs={{0,1},{1,0},{2,3},{3,2},{4,5},{5,4},{6,7},{7,6},{8,9},{9,8},{10,11... | collective-permute-start | bytes 196616 | tf_op jit(solution)/shard_map/ppermute | solution.py:16
Sparse Core Ops, SparseCore 0:
  9.6 48.6 all-gather.5
  60.1 26.5 all-gather.3
  93.7 41.2 reduce-scatter.1
where the time goes:
time: 144 us
  waiting for transfers between devices  113 us (78%)
  between operations  13.8 us (10%)
  matrix products  7.24 us (5%)
  local copies, waits for them, and re-layouts  3.77 us (3%)
  other arithmetic  3.15 us (2%)
  starting transfers between devices  2.2 us (2%)
    all_gather x1, waiting for transfers between devices, local(): grad_full = lax.all_gather(grad_local, 'tensor', axis=0, tiled=True)  47.4 us
    reduce_scatter x1, waiting for transfers between devices, local(): lax.psum_scatter(lax.dot_general(columns, flat_out, (((0,), (0,)), ((), (...  33 us
    all_gather x1, waiting for transfers between devices, local(): lax.all_gather(out_weight, 'dp', axis=0, tiled=True)  28.5 us
    dot_general x1, matrix products, local(): jnp.dot(columns, lax.all_gather(out_weight, 'dp', axis=0, tiled=True), pr...  3.15 us
    ppermute x2, waiting for transfers between devices, from_partner(): return lax.ppermute(block, axis, route)  3.08 us
  transfers between devices with their start and end apart: 5, of which 5 were waited for; matrix products, arithmetic and copies ran while one was open for 4% of the time, Pallas kernels for 0%

commit v1 on v0

--- a/solution.py
+++ b/solution.py
@@ -4,6 +4,33 @@
 from jax.sharding import PartitionSpec as P
 
 HD = 128
+
+
+def supply_all_vectors(tile_in, k_dim):
+    then = list(tile_in.shape[1:])
+    then[k_dim] *= tile_in.shape[0]
+    return jnp.moveaxis(tile_in, 0, k_dim).reshape(then)
+
+
+def turn_group_on(own_rows, peer_axis, at_axis):
+    how_many = jax.lax.axis_size(peer_axis)
+    runs = tuple(((t, (t + 1) % how_many) for t in range(how_many)))
+    windows = tuple(((num, it) for it, num in runs))
+    piece_next, aux = ([], [])
+    tick = 0
+    while tick < how_many - 1:
+        if tick % 2 == 0:
+            item_now = jax.lax.ppermute(piece_next[-1] if piece_next else own_rows, peer_axis, runs)
+            piece_next.append(item_now)
+        else:
+            u_next = jax.lax.ppermute(aux[-1] if aux else own_rows, peer_axis, windows)
+            aux.append(u_next)
+        tick = tick + 1
+    piece_now = jnp.stack([*piece_next[::-1], own_rows, *aux])
+    arr_next = jax.lax.axis_index(peer_axis)
+    big = arr_next - len(piece_next)
+    piece_now = piece_now[(jnp.arange(how_many) - big) % how_many]
+    return supply_all_vectors(piece_now, at_axis)
 
 
 def from_partner(block, axis, bit):
@@ -45,9 +72,7 @@
     grad_full = lax.all_gather(grad_local, "tensor", axis=0, tiled=True)
     columns = grad_full
     grad_sum = jnp.dot(
-        columns,
-        lax.all_gather(out_weight, "dp", axis=0, tiled=True),
-        preferred_element_type=jnp.float32,
+        columns, turn_group_on(out_weight, "dp", 0), preferred_element_type=jnp.float32
     )
     columns = grad_full
     weight_rows = lax.psum_scatter(

time: 144 us -> 114 us (0.79)
  waiting for transfers between devices: 113 us -> 68.2 us
  starting transfers between devices: 2.2 us -> 10.6 us
  local copies, waits for them, and re-layouts: 3.77 us -> 9.88 us
    all_gather x1, waiting for transfers between devices: 47.4 us -> 13.8 us  [local(): grad_full = lax.all_gather(grad_local, 'tensor', axis=0, tiled=True)]
    all_gather x1 -> x0, waiting for transfers between devices: 28.5 us -> none  [local(): lax.all_gather(out_weight, 'dp', axis=0, tiled=True)]
    ppermute x0 -> x7, waiting for transfers between devices: none -> 20 us  [the longest x4 20 us: turn_group_on(): jax.lax.ppermute(piece_next[-1] if piece_next else own_rows, peer_axis, r...]
    ppermute x0 -> x7, starting transfers between devices: none -> 8.38 us  [the longest x3 7.87 us: turn_group_on(): u_next = jax.lax.ppermute(aux[-1] if aux else own_rows, peer_axis, windows)]
    unnamed x8 -> x21, local copies, waits for them, and re-layouts: 2.83 us -> 6.83 us
    gather x0 -> x1, local copies, waits for them, and re-layouts: none -> 1.99 us  [turn_group_on(): piece_now = piece_now[(jnp.arange(how_many) - big) % how_many]]
    ppermute x2, waiting for transfers between devices: 3.08 us -> 1.12 us  [from_partner(): return lax.ppermute(block, axis, route)]
  transfers between devices with their start and end apart: 5 -> 11, of which waited for: 5 -> 8; matrix products, arithmetic and copies ran while one was open for 4% -> 10% of each run, Pallas kernels for 0% -> 0%
where the time goes in v1:
time: 114 us
  waiting for transfers between devices  68.2 us (60%)
  between operations  14.2 us (12%)
  starting transfers between devices  10.6 us (9%)
  local copies, waits for them, and re-layouts  9.88 us (9%)
  matrix products  7.86 us (7%)
  other arithmetic  3.16 us (3%)
    reduce_scatter x1, waiting for transfers between devices, local(): lax.psum_scatter(lax.dot_general(columns, flat_out, (((0,), (0,)), ((), (...  32.6 us
    ppermute x4, waiting for transfers between devices, turn_group_on(): jax.lax.ppermute(piece_next[-1] if piece_next else own_rows, peer_axis, r...  20 us
    all_gather x1, waiting for transfers between devices, local(): grad_full = lax.all_gather(grad_local, 'tensor', axis=0, tiled=True)  13.8 us
    ppermute x3, starting transfers between devices, turn_group_on(): u_next = jax.lax.ppermute(aux[-1] if aux else own_rows, peer_axis, windows)  7.87 us
    unnamed x21, local copies, waits for them, and re-layouts  6.83 us
    dot_general x1, matrix products, local(): jnp.dot(columns, turn_group_on(out_weight, 'dp', 0), preferred_element_ty...  3.01 us
  transfers between devices with their start and end apart: 11, of which 8 were waited for; matrix products, arithmetic and copies ran while one was open for 10% of the time, Pallas kernels for 0%

profile of v1, /device:TPU:0, one launch (start us, length us, event | category | flops | bytes accessed | tf_op | source)
XLA Modules:
  0.0 113.9 jit_solution(6546431213387021698)
XLA Ops:
  7.2 0.0 copy-start
  7.2 0.0 copy-start.2
  7.2 0.0 all-gather.3.cloned.1.call-start
  7.2 0.7 all-gather.3.cloned.1.call-update
  7.9 0.0 reduce-scatter.2.cloned.1.call-start
  8.0 0.5 collective-permute-start
  8.5 7.1 %collective-permute-done = bf16[512,256]{1,0:T(8,128)(2,1)S(1)} collective-permute-done((bf16[512,256]{1,0:T(8,128)(2,1)}, bf16[512,256]{1,0:T(8,128)(2,1)S(1)}, u32[]{:S(2)}, u32[]{:S(2)}) %collective-permute-start) | collective-permute-done | bytes 262176 | tf_op jit(solution)/shard_map/ppermute | solution.py:23
  15.6 0.0 collective-permute-start.1
  15.6 2.6 %collective-permute-start.4 = (bf16[512,256]{1,0:T(8,128)(2,1)}, bf16[512,256]{1,0:T(8,128)(2,1)S(1)}, u32[]{:S(2)}, u32[]{:S(2)}) collective-permute-start(bf16[512,256]{1,0:T(8,128)(2,1)} %param.7), channel_id=1, source_target_pairs={{4,0},{8,4},{12,8},{16,12},{20,16},{24,20},{28,24},{0,28},{5,1},{9... | collective-permute-start | bytes 786440 | tf_op jit(solution)/shard_map/ppermute | solution.py:26
  18.3 4.9 %collective-permute-done.1 = bf16[512,256]{1,0:T(8,128)(2,1)S(1)} collective-permute-done((bf16[512,256]{1,0:T(8,128)(2,1)S(1)}, bf16[512,256]{1,0:T(8,128)(2,1)S(1)}, u32[]{:S(2)}, u32[]{:S(2)}) %collective-permute-start.1) | collective-permute-done | bytes 262176 | tf_op jit(solution)/shard_map/ppermute | solution.py:23
  23.2 0.0 collective-permute-start.2
  23.2 0.9 fusion.16
  24.0 0.0 collective-permute-done.4
  24.0 2.7 %collective-permute-start.5 = (bf16[512,256]{1,0:T(8,128)(2,1)S(1)}, bf16[512,256]{1,0:T(8,128)(2,1)}, u32[]{:S(2)}, u32[]{:S(2)}) collective-permute-start(bf16[512,256]{1,0:T(8,128)(2,1)S(1)} %collective-permute-done.4), channel_id=1, source_target_pairs={{4,0},{8,4},{12,8},{16,12},{20,16},{24,20},{28,24},{0,28},{5,1},{9... | collective-permute-start | bytes 786440 | tf_op jit(solution)/shard_map/ppermute | solution.py:26
  26.7 4.4 %collective-permute-done.2 = bf16[512,256]{1,0:T(8,128)(2,1)S(1)} collective-permute-done((bf16[512,256]{1,0:T(8,128)(2,1)S(1)}, bf16[512,256]{1,0:T(8,128)(2,1)S(1)}, u32[]{:S(2)}, u32[]{:S(2)}) %collective-permute-start.2) | collective-permute-done | bytes 262176 | tf_op jit(solution)/shard_map/ppermute | solution.py:23
  31.1 0.0 collective-permute-start.3
  31.1 1.0 reshape_squeeze.3
  32.2 0.0 copy-done
  32.2 1.1 fusion.57
  33.3 0.0 collective-permute-done.5
  33.3 2.5 %collective-permute-start.6 = (bf16[512,256]{1,0:T(8,128)(2,1)}, bf16[512,256]{1,0:T(8,128)(2,1)S(1)}, u32[]{:S(2)}, u32[]{:S(2)}) collective-permute-start(bf16[512,256]{1,0:T(8,128)(2,1)} %collective-permute-done.5), channel_id=1, source_target_pairs={{4,0},{8,4},{12,8},{16,12},{20,16},{24,20},{28,24},{0,28},{5,1},{9... | collective-permute-start | bytes 786440 | tf_op jit(solution)/shard_map/ppermute | solution.py:26
  35.8 3.6 %collective-permute-done.3 = bf16[512,256]{1,0:T(8,128)(2,1)} collective-permute-done((bf16[512,256]{1,0:T(8,128)(2,1)S(1)}, bf16[512,256]{1,0:T(8,128)(2,1)}, u32[]{:S(2)}, u32[]{:S(2)}) %collective-permute-start.3) | collective-permute-done | bytes 262176 | tf_op jit(solution)/shard_map/ppermute | solution.py:23
  39.4 1.0 bitcast_dynamic-update-slice_fusion.7
  40.4 1.0 bitcast_dynamic-update-slice_fusion.6
  41.5 1.0 bitcast_dynamic-update-slice_fusion.1
  42.5 0.0 collective-permute-done.6
  42.5 2.0 %gather_fusion = bf16[8,512,256]{2,1,0:T(8,128)(2,1)} fusion(bf16[8,512,256]{2,1,0:T(8,128)(2,1)S(1)} %bitcast_dynamic-update-slice_fusion, s32[1024]{0:T(1024)S(1)} %pad_clamp_fusion), kind=kCustom, calls=%fused_computation | custom fusion | bytes 4194336 | tf_op jit(solution)/shard_map/gather | solution.py:32
  44.5 13.8 %all-gather.3.cloned.1.call-done = bf16[1,256,4096]{2,1,0:T(8,128)(2,1)} async-done(((bf16[1,64,4096]{2,1,0:T(8,128)(2,1)}), bf16[1,256,4096]{2,1,0:T(8,128)(2,1)}) %all-gather.3.cloned.1.call-update) | async-done | bytes 2097168 | tf_op jit(solution)/shard_map/all_gather | solution.py:72
  58.3 3.0 %fusion.13 = bf16[256,256]{1,0:T(8,128)(2,1)S(1)} fusion(bf16[4096,256]{1,0:T(8,128)(2,1)} %bitcast.123, bf16[1,256,4096]{2,1,0:T(8,128)(2,1)} %all-gather.3.cloned.1.call-done), kind=kOutput, calls=%fused_computation.19 | convolution fusion | flops 536936448 | bytes 4325376 | tf_op jit(solution)/shard_map/dot_general | solution.py:74
  61.3 0.5 multiply_reduce_fusion
  61.8 1.0 copy-done.1
  62.9 2.1 %fusion.1 = bf16[4096,256]{0,1:T(8,128)(2,1)} fusion(bf16[256,256]{0,1:T(8,128)(2,1)S(1)} %bitcast.125, bf16[1,256,4096]{2,1,0:T(8,128)(2,1)S(1)} %copy-done.1), kind=kOutput, calls=%fused_computation.3 | convolution fusion | flops 537919488 | bytes 4325376 | tf_op jit(solution)/shard_map/dot_general | solution.py:79
  64.9 0.0 reduce-scatter.2.cloned.1.call-update
  65.0 1.0 copy-done.5
  66.0 0.2 fusion.12
  66.2 0.2 fusion.66
  66.4 0.1 collective-permute-start.7
  66.5 0.2 convolution_convert_fusion.1
  66.7 0.5 fusion.67
  67.3 2.1 %collective-permute-start.8 = (bf16[256,128]{1,0:T(8,128)(2,1)S(1)}, bf16[256,128]{1,0:T(8,128)(2,1)S(1)}, u32[]{:S(2)}, u32[]{:S(2)}) collective-permute-start(bf16[256,128]{1,0:T(8,128)(2,1)S(1)} %get-tuple-element.14), channel_id=1, source_target_pairs={{0,1},{1,0},{2,3},{3,2},{4,5},{5,4},{6,7},{7,6},{8,9},{9,8},{10,11... | collective-permute-start | bytes 196616 | tf_op jit(solution)/shard_map/ppermute | solution.py:43
  69.3 0.8 copy.19
  70.1 1.1 collective-permute-done.7
  71.2 0.6 fusion.20
  71.8 0.1 collective-permute-done.8
  71.9 0.6 fusion.21
  72.5 32.6 %reduce-scatter.2.cloned.1.call-done = bf16[512,256]{0,1:T(8,128)(2,1)} async-done(((bf16[4096,256]{0,1:T(8,128)(2,1)}), bf16[512,256]{0,1:T(8,128)(2,1)}) %reduce-scatter.2.cloned.1.call-update) | async-done | bytes 262160 | tf_op jit(solution)/shard_map/reduce_scatter | solution.py:78
  105.1 1.0 convert_multiply_fusion
  106.1 1.0 copy.20
  (14 shorter events, 0.1 us)
Async XLA Ops:
  7.2 25.0 %copy-start = (bf16[1,256,128]{2,1,0:T(8,128)(2,1)S(1)}, bf16[1,256,128]{2,1,0:T(8,128)(2,1)}, u32[]{:S(2)}) copy-start(bf16[1,256,128]{2,1,0:T(8,128)(2,1)} %param.9) | copy-start | bytes 196612
  7.2 34.3 %copy-start.2 = (bf16[512,256]{1,0:T(8,128)(2,1)S(1)}, bf16[512,256]{1,0:T(8,128)(2,1)}, u32[]{:S(2)}) copy-start(bf16[512,256]{1,0:T(8,128)(2,1)} %param.7) | copy-start | bytes 786436
  7.2 51.1 %all-gather.3.cloned.1.call-start = ((), (), s32[]{:S(2)}) async-start(), calls=%async_computation.2 | async-start | bytes 2621440 | tf_op jit(solution)/shard_map/all_gather | solution.py:72
  7.9 97.1 %reduce-scatter.2.cloned.1.call-start = ((), (), s32[]{:S(2)}) async-start(), calls=%async_computation.1 | async-start | bytes 2359296 | tf_op jit(solution)/shard_map/reduce_scatter | solution.py:78
  8.0 7.7 %collective-permute-start = (bf16[512,256]{1,0:T(8,128)(2,1)}, bf16[512,256]{1,0:T(8,128)(2,1)S(1)}, u32[]{:S(2)}, u32[]{:S(2)}) collective-permute-start(bf16[512,256]{1,0:T(8,128)(2,1)} %param.7), channel_id=1, source_target_pairs={{0,4},{4,8},{8,12},{12,16},{16,20},{20,24},{24,28},{28,0},{1,5},{5... | collective-permute-start | bytes 786440 | tf_op jit(solution)/shard_map/ppermute | solution.py:23
  15.6 7.5 %collective-permute-start.1 = (bf16[512,256]{1,0:T(8,128)(2,1)S(1)}, bf16[512,256]{1,0:T(8,128)(2,1)S(1)}, u32[]{:S(2)}, u32[]{:S(2)}) collective-permute-start(bf16[512,256]{1,0:T(8,128)(2,1)S(1)} %collective-permute-done), channel_id=1, source_target_pairs={{0,4},{4,8},{8,12},{12,16},{16,20},{20,24},{24,28},{28,0},{1,5},{5... | collective-permute-start | bytes 786440 | tf_op jit(solution)/shard_map/ppermute | solution.py:23
  15.6 8.4 %collective-permute-start.4 = (bf16[512,256]{1,0:T(8,128)(2,1)}, bf16[512,256]{1,0:T(8,128)(2,1)S(1)}, u32[]{:S(2)}, u32[]{:S(2)}) collective-permute-start(bf16[512,256]{1,0:T(8,128)(2,1)} %param.7), channel_id=1, source_target_pairs={{4,0},{8,4},{12,8},{16,12},{20,16},{24,20},{28,24},{0,28},{5,1},{9... | collective-permute-start | bytes 786440 | tf_op jit(solution)/shard_map/ppermute | solution.py:26
  23.2 8.0 %collective-permute-start.2 = (bf16[512,256]{1,0:T(8,128)(2,1)S(1)}, bf16[512,256]{1,0:T(8,128)(2,1)S(1)}, u32[]{:S(2)}, u32[]{:S(2)}) collective-permute-start(bf16[512,256]{1,0:T(8,128)(2,1)S(1)} %collective-permute-done.1), channel_id=1, source_target_pairs={{0,4},{4,8},{8,12},{12,16},{16,20},{20,24},{24,28},{28,0},{1,5},{5... | collective-permute-start | bytes 786440 | tf_op jit(solution)/shard_map/ppermute | solution.py:23
  24.0 9.2 %collective-permute-start.5 = (bf16[512,256]{1,0:T(8,128)(2,1)S(1)}, bf16[512,256]{1,0:T(8,128)(2,1)}, u32[]{:S(2)}, u32[]{:S(2)}) collective-permute-start(bf16[512,256]{1,0:T(8,128)(2,1)S(1)} %collective-permute-done.4), channel_id=1, source_target_pairs={{4,0},{8,4},{12,8},{16,12},{20,16},{24,20},{28,24},{0,28},{5,1},{9... | collective-permute-start | bytes 786440 | tf_op jit(solution)/shard_map/ppermute | solution.py:26
  31.1 4.7 %copy-start.3 = (bf16[512,256]{1,0:T(8,128)(2,1)}, bf16[512,256]{1,0:T(8,128)(2,1)S(1)}, u32[]{:S(2)}) copy-start(bf16[512,256]{1,0:T(8,128)(2,1)S(1)} %collective-permute-done.2) | copy-start | bytes 786436
  31.1 8.3 %collective-permute-start.3 = (bf16[512,256]{1,0:T(8,128)(2,1)S(1)}, bf16[512,256]{1,0:T(8,128)(2,1)}, u32[]{:S(2)}, u32[]{:S(2)}) collective-permute-start(bf16[512,256]{1,0:T(8,128)(2,1)S(1)} %collective-permute-done.2), channel_id=1, source_target_pairs={{0,4},{4,8},{8,12},{12,16},{16,20},{20,24},{24,28},{28,0},{1,5},{5... | collective-permute-start | bytes 786440 | tf_op jit(solution)/shard_map/ppermute | solution.py:23
  33.3 9.2 %collective-permute-start.6 = (bf16[512,256]{1,0:T(8,128)(2,1)}, bf16[512,256]{1,0:T(8,128)(2,1)S(1)}, u32[]{:S(2)}, u32[]{:S(2)}) collective-permute-start(bf16[512,256]{1,0:T(8,128)(2,1)} %collective-permute-done.5), channel_id=1, source_target_pairs={{4,0},{8,4},{12,8},{16,12},{20,16},{24,20},{28,24},{0,28},{5,1},{9... | collective-permute-start | bytes 786440 | tf_op jit(solution)/shard_map/ppermute | solution.py:26
  58.3 3.0 %copy-start.4 = (bf16[1,256,128]{2,1,0:T(8,128)(2,1)S(1)}, bf16[1,256,128]{2,1,0:T(8,128)(2,1)}, u32[]{:S(2)}) copy-start(bf16[1,256,128]{2,1,0:T(8,128)(2,1)} %param.10) | copy-start | bytes 196612
  61.3 1.6 %copy-start.1 = (bf16[1,256,4096]{2,1,0:T(8,128)(2,1)S(1)}, bf16[1,256,4096]{2,1,0:T(8,128)(2,1)}, u32[]{:S(2)}) copy-start(bf16[1,256,4096]{2,1,0:T(8,128)(2,1)} %all-gather.3.cloned.1.call-done) | copy-start | bytes 6291460
  64.9 1.0 copy-start.5
  66.4 4.7 %collective-permute-start.7 = (bf16[256,128]{1,0:T(8,128)(2,1)S(1)}, bf16[256,128]{1,0:T(8,128)(2,1)S(1)}, u32[]{:S(2)}, u32[]{:S(2)}) collective-permute-start(bf16[256,128]{1,0:T(8,128)(2,1)S(1)} %get-tuple-element.12), channel_id=1, source_target_pairs={{0,1},{1,0},{2,3},{3,2},{4,5},{5,4},{6,7},{7,6},{8,9},{9,8},{10,11... | collective-permute-start | bytes 196616 | tf_op jit(solution)/shard_map/ppermute | solution.py:43
  67.3 4.6 %collective-permute-start.8 = (bf16[256,128]{1,0:T(8,128)(2,1)S(1)}, bf16[256,128]{1,0:T(8,128)(2,1)S(1)}, u32[]{:S(2)}, u32[]{:S(2)}) collective-permute-start(bf16[256,128]{1,0:T(8,128)(2,1)S(1)} %get-tuple-element.14), channel_id=1, source_target_pairs={{0,1},{1,0},{2,3},{3,2},{4,5},{5,4},{6,7},{7,6},{8,9},{9,8},{10,11... | collective-permute-start | bytes 196616 | tf_op jit(solution)/shard_map/ppermute | solution.py:43
Sparse Core Ops, SparseCore 0:
  9.6 48.6 all-gather.2
  65.1 39.9 reduce-scatter.1
